TPU v7x, 32 devices: a whole 2x2x4 slice. The times are simulated.
32 devices in a mesh: parts: 1, ctx: 4 (over z), pb: 4 (over y, x), row: 2 (over core).
Axes of the slice: x: 2, y: 2, z: 4, core: 2. Of those that a mesh axis runs over, the one named last changes fastest.
Arguments:
- queries: bfloat16 [2048, 3072], P(('parts', 'ctx', 'pb', 'row')), may hold values from -10 to 10
- cache_keys: bfloat16 [4096, 192], P(('parts', 'ctx')), may hold values from -10 to 10
- cache_values: bfloat16 [4096, 128], P(('parts', 'ctx')), may hold values from -6 to 6
- span_keys: bfloat16 [2048, 192], P(('parts', 'ctx')), may hold values from -10 to 10
- span_values: bfloat16 [2048, 128], P(('parts', 'ctx')), may hold values from -6 to 6
- pool_keys: float32 [32, 192], replicated, may hold values from 0.2 to 0.6
- pool_values: float32 [32, 128], replicated, may hold values from 0.05 to 0.3
- gate_logits: bfloat16 [2048, 48], P(('parts', 'ctx', 'pb', 'row')), may hold values from -6 to 6
- chosen_blocks: int32 [32, 16], P(('parts', 'ctx', 'pb', 'row')), may hold values from 0 to 95, as said below
- valid_counts: int32 [32], P(('parts', 'ctx', 'pb', 'row')), may hold values from 4 to 16
Outputs:
- mixed: bfloat16 [2048, 2048], P(('parts', 'ctx', 'pb', 'row'))
Inputs may be any that keep to these rules, and one draw needn't show every extreme that they name: `chosen_blocks`: slot 0 of tile t holds the tile's own block 64 + t. Slot s > 0 holds a block of the cache stored by ctx index (c + s) mod (4), where c is the ctx index that holds tile t; the blocks of one tile are distinct. Slots at or beyond the tile's valid count hold blocks too and are ignored.
All inputs are finite; a program needn't handle non-finite values.
Results may differ from a plain program's by a relative error of at most 0.0034.
The roundings to bfloat16 on the way count: a program that leaves them out, or rounds other values in their place, can miss the bound.
Values may be sent and summed in bfloat16 or wider, within the bound.
A program may use at most 64 MiB of HBM per device.

v0:
```python
import math
import jax
import jax.numpy as jnp
from jax import lax
from jax.sharding import PartitionSpec as P

HEADS = 16
CLEN = 32
STRIDE = 16
BLOCK = 64
WINDOW = 256
NEG_FILL = -1e30


def from_behind(value, axis, steps):
    count = lax.axis_size(axis)
    pairs = [(source, (source + steps) % count) for source in range(count)]
    return lax.ppermute(value, axis, pairs)


def pool_blocks(rows, extra, weights, stride):
    joined = jnp.concatenate([rows, extra], axis=0).astype(jnp.float32)
    blocks = rows.shape[0] // stride
    grouped = joined.reshape(blocks + 1, stride, rows.shape[1])
    leading = jnp.sum(grouped[:-1] * weights[None, :stride, :], axis=1)
    trailing = jnp.sum(grouped[1:] * weights[None, stride:, :], axis=1)
    return (leading + trailing).astype(jnp.bfloat16)


def attend(query_rows, keys, values, visible, score_scale):
    scores = jnp.dot(query_rows, keys.T, preferred_element_type=jnp.float32) * score_scale
    scores = jnp.where(visible, scores, NEG_FILL)
    highest = jnp.max(scores, axis=1, keepdims=True)
    exponent = jnp.where(visible, jnp.exp(scores - highest), 0.0)
    weights = exponent.astype(jnp.bfloat16)
    numerator = jnp.dot(weights, values, preferred_element_type=jnp.float32)
    return numerator / jnp.sum(exponent, axis=1, keepdims=True)


def local(
    queries,
    cache_keys,
    cache_values,
    span_keys,
    span_values,
    pool_keys,
    pool_values,
    gate_logits,
    chosen_blocks,
    valid_counts,
):
    owners = lax.axis_size("ctx")
    ctx_place = lax.axis_index("ctx")
    tile_place = lax.axis_index("pb") * lax.axis_size("row") + lax.axis_index("row")
    cache_len, key_width = cache_keys.shape
    value_width = cache_values.shape[1]
    span_len = span_keys.shape[0]
    tokens = queries.shape[0]
    tiles_here = chosen_blocks.shape[0]
    score_scale = 1.0 / math.sqrt(key_width)
    context_start = cache_len * owners
    local_start = tile_place * tokens
    first_pos = context_start + ctx_place * span_len + local_start
    row_count = tokens * HEADS
    query_rows = queries.reshape(row_count, key_width)
    row_pos = first_pos + jnp.arange(row_count, dtype=jnp.int32) // HEADS
    leader = ctx_place == 0
    outgoing = (
        jnp.where(leader, span_keys[:STRIDE], cache_keys[:STRIDE]),
        jnp.where(leader, span_values[:STRIDE], cache_values[:STRIDE]),
        span_keys[:STRIDE],
        span_values[:STRIDE],
    )
    heads_next = from_behind((outgoing[0], outgoing[1], outgoing[2], outgoing[3]), "ctx", -1)
    summary_keys = jnp.concatenate(
        [
            pool_blocks(cache_keys, heads_next[0], pool_keys, STRIDE),
            pool_blocks(span_keys, heads_next[2], pool_keys, STRIDE),
        ],
        axis=0,
    )
    summary_values = jnp.concatenate(
        [
            pool_blocks(cache_values, heads_next[1], pool_values, STRIDE),
            pool_blocks(span_values, heads_next[3], pool_values, STRIDE),
        ],
        axis=0,
    )
    cache_blocks = cache_len // STRIDE
    span_blocks = span_len // STRIDE
    per_ctx = cache_blocks + span_blocks
    first_row = jnp.int32(0)
    running_max = jnp.full((row_count,), NEG_FILL, jnp.float32)
    running_sum = jnp.zeros((row_count,), jnp.float32)
    running_out = jnp.zeros((row_count, value_width), jnp.float32)
    part_keys = lax.all_gather(summary_keys, "ctx", axis=0, tiled=True)
    part_values = lax.all_gather(summary_values, "ctx", axis=0, tiled=True)
    length = part_keys.shape[0]
    for lower_row in range(0, length, 512):
        upper_row = min(lower_row + 512, length)
        block_index = first_row + lower_row + jnp.arange(upper_row - lower_row, dtype=jnp.int32)
        owner_of = block_index // per_ctx
        within = block_index % per_ctx
        block_id = jnp.where(
            within < cache_blocks,
            owner_of * cache_blocks + within,
            owners * cache_blocks + owner_of * span_blocks + within - cache_blocks,
        )
        visible = (block_id * STRIDE + CLEN)[None, :] <= row_pos[:, None] + 1
        scores = (
            jnp.dot(
                query_rows, part_keys[lower_row:upper_row].T, preferred_element_type=jnp.float32
            )
            * score_scale
        )
        scores = jnp.where(visible, scores, NEG_FILL)
        new_max = jnp.maximum(running_max, jnp.max(scores, axis=1))
        exponent = jnp.where(visible, jnp.exp(scores - new_max[:, None]), 0.0)
        fading = jnp.exp(running_max - new_max)
        running_sum = running_sum * fading + jnp.sum(exponent, axis=1)
        running_out = running_out * fading[:, None] + jnp.dot(
            exponent.astype(jnp.bfloat16),
            part_values[lower_row:upper_row],
            preferred_element_type=jnp.float32,
        )
        running_max = new_max
    summary_out = running_out / running_sum[:, None]
    reach = chosen_blocks.shape[1] // owners
    arranged = chosen_blocks.reshape(tiles_here, reach, owners)
    column_of = (jnp.arange(owners, dtype=jnp.int32) - ctx_place) % owners
    requested = jnp.take(arranged, column_of, axis=2)
    wanted = lax.all_to_all(requested, "ctx", split_axis=2, concat_axis=2, tiled=True)
    cache_count = cache_len // BLOCK
    span_count = span_len // BLOCK
    from_cache = (wanted < owners * cache_count)[..., None, None]
    cache_slot = jnp.clip(wanted - ctx_place * cache_count, 0, cache_count - 1)
    span_slot = jnp.clip(wanted - owners * cache_count - ctx_place * span_count, 0, span_count - 1)
    served_keys = jnp.where(
        from_cache,
        cache_keys.reshape(cache_count, BLOCK, key_width)[cache_slot],
        span_keys.reshape(span_count, BLOCK, key_width)[span_slot],
    )
    served_values = jnp.where(
        from_cache,
        cache_values.reshape(cache_count, BLOCK, value_width)[cache_slot],
        span_values.reshape(span_count, BLOCK, value_width)[span_slot],
    )
    fetched_keys, fetched_values = (
        lax.all_to_all(served_keys, "ctx", split_axis=2, concat_axis=2, tiled=True),
        lax.all_to_all(served_values, "ctx", split_axis=2, concat_axis=2, tiled=True),
    )
    last_ctx = ctx_place == owners - 1
    tail_rows = from_behind(
        (
            jnp.where(last_ctx, cache_keys[-WINDOW:], span_keys[-WINDOW:]),
            jnp.where(last_ctx, cache_values[-WINDOW:], span_values[-WINDOW:]),
        ),
        "ctx",
        1,
    )
    reach_keys = jnp.concatenate([tail_rows[0], span_keys], axis=0)
    reach_values = jnp.concatenate([tail_rows[1], span_values], axis=0)
    gate_values = jax.nn.sigmoid(gate_logits.astype(jnp.float32)).reshape(tokens, 3, HEADS)
    offsets = jnp.arange(BLOCK, dtype=jnp.int32)
    near_offsets = jnp.arange(WINDOW + BLOCK, dtype=jnp.int32)
    slot_number = jnp.arange(reach, dtype=jnp.int32)[:, None] * owners + column_of[None, :]
    key_pos = (requested[0][:, :, None] * BLOCK + offsets).reshape(-1)
    usable = jnp.repeat((slot_number < valid_counts[0]).reshape(-1), BLOCK)
    sel_visible = usable[None, :] & (key_pos[None, :] <= row_pos[:, None])
    picked = attend(
        query_rows,
        fetched_keys[0].reshape(-1, key_width),
        fetched_values[0].reshape(-1, value_width),
        sel_visible,
        score_scale,
    )
    begin = local_start + 0
    near_keys = lax.dynamic_slice_in_dim(reach_keys, begin, WINDOW + BLOCK, 0)
    near_values = lax.dynamic_slice_in_dim(reach_values, begin, WINDOW + BLOCK, 0)
    near_pos = context_start + ctx_place * span_len - WINDOW + begin + near_offsets
    near_visible = (near_pos[None, :] <= row_pos[:, None]) & (
        near_pos[None, :] > row_pos[:, None] - WINDOW
    )
    nearby = attend(query_rows, near_keys, near_values, near_visible, score_scale)
    mixed = (
        gate_values[:, 0, :, None] * summary_out.reshape(BLOCK, HEADS, value_width)
        + gate_values[:, 1, :, None] * picked.reshape(BLOCK, HEADS, value_width)
        + gate_values[:, 2, :, None] * nearby.reshape(BLOCK, HEADS, value_width)
    )
    outputs = mixed.reshape(BLOCK, HEADS * value_width).astype(jnp.bfloat16)
    return outputs


def solution(mesh):
    return jax.shard_map(
        local,
        mesh=mesh,
        in_specs=(
            P(("parts", "ctx", "pb", "row"), None),
            P(("parts", "ctx"), None),
            P(("parts", "ctx"), None),
            P(("parts", "ctx"), None),
            P(("parts", "ctx"), None),
            P(),
            P(),
            P(("parts", "ctx", "pb", "row"), None),
            P(("parts", "ctx", "pb", "row"), None),
            P(("parts", "ctx", "pb", "row")),
        ),
        out_specs=P(("parts", "ctx", "pb", "row"), None),
        check_vma=False,
    )
```

profile of v0, /device:TPU:0, one launch (start us, length us, event | category | flops | bytes accessed | tf_op | source)
XLA Modules:
  0.0 91.8 jit_solution(5316688061465802636)
XLA Ops:
  0.0 1.3 %copy.79 = bf16[1024,192]{1,0:T(8,128)(2,1)S(1)} copy(bf16[1024,192]{0,1:T(8,128)(2,1)} %param.11) | data formatting | bytes 786432 | tf_op args[1]
  1.3 1.1 %copy.77 = bf16[512,192]{1,0:T(8,128)(2,1)S(1)} copy(bf16[512,192]{0,1:T(8,128)(2,1)} %param.13) | data formatting | bytes 393216 | tf_op args[3]
  3.0 5.1 %collective-permute-start = (bf16[16,192]{1,0:T(8,128)(2,1)}, bf16[16,192]{1,0:T(8,128)(2,1)}, u32[]{:S(2)}, u32[]{:S(2)}) collective-permute-start(bf16[16,192]{1,0:T(8,128)(2,1)} %get-tuple-element.13), channel_id=1, source_target_pairs={{0,24},{8,0},{16,8},{24,16},{1,25},{9,1},{17,9},{25,17},{2,26},{10... | collective-permute-start | bytes 18440 | tf_op jit(solution)/shard_map/ppermute | solution.py:18
  8.5 1.3 %slice_select_fusion.3 = (bf16[16,128]{1,0:T(8,128)(2,1)}, bf16[16,128]{1,0:T(8,128)(2,1)}) fusion(bf16[1024,128]{1,0:T(8,128)(2,1)} %param.12, pred[]{:T(512)S(6)} %eq.10, bf16[512,128]{1,0:T(8,128)(2,1)} %param.14), kind=kLoop, calls=%fused_computation.87 | loop fusion | flops 2048 | bytes 16385 | tf_op jit(solution)/shard_map/jit(_where)/select_n | solution.py:70
  10.8 1.3 %reduce.3 = s32[16]{0:T(128)S(1)} reduce(s32[1,16]{1,0:T(1,128)} %param.18, s32[]{:T(128)} %broadcast.494), dimensions={0}, to_apply=%param.18.reduce_sub_computation.3 | reduce | bytes 132 | tf_op args[8]
  13.7 5.3 %all-to-all-start = ((s32[1,4,4]{1,0,2:T(1,128)}), s32[1,4,4]{1,0,2:T(1,128)S(1)}, u32[]{:S(2)}, u32[]{:S(2)}) async-start(s32[1,4,4]{1,0,2:T(1,128)} %copy.85), calls=%async_computation | async-start | bytes 4096 | tf_op jit(solution)/shard_map/all_to_all | solution.py:132
  18.9 1.0 %slice_select_fusion = bf16[256,192]{0,1:T(8,128)(2,1)S(1)} fusion(bf16[512,192]{0,1:T(8,128)(2,1)} %param.13, bf16[1024,192]{0,1:T(8,128)(2,1)} %param.11, pred[]{:T(512)S(6)} %eq.11), kind=kLoop, calls=%fused_computation.60 | loop fusion | flops 49152 | bytes 294913 | tf_op jit(solution)/shard_map/jit(_where)/select_n | solution.py:155
  19.9 2.1 %collective-permute-start.4 = (bf16[256,192]{0,1:T(8,128)(2,1)S(1)}, bf16[256,192]{0,1:T(8,128)(2,1)}, u32[]{:S(2)}, u32[]{:S(2)}) collective-permute-start(bf16[256,192]{0,1:T(8,128)(2,1)S(1)} %slice_select_fusion), channel_id=1, source_target_pairs={{0,8},{8,16},{16,24},{24,0},{1,9},{9,17},{17,25},{25,1},{2,10},{10... | collective-permute-start | bytes 294920 | tf_op jit(solution)/shard_map/ppermute | solution.py:18
  30.3 0.7 copy.95
  31.1 3.6 %all-to-all-start.2 = ((bf16[1,4,4,64,128]{4,3,1,0,2:T(8,128)(2,1)}), bf16[1,4,4,64,128]{4,3,1,0,2:T(8,128)(2,1)S(1)}, u32[]{:S(2)}, u32[]{:S(2)}) async-start(bf16[1,4,4,64,128]{4,3,1,0,2:T(8,128)(2,1)} %copy.95), calls=%async_computation.2 | async-start | bytes 524288 | tf_op jit(solution)/shard_map/all_to_all | solution.py:150
  34.7 0.9 copy_select_fusion
  35.6 2.0 %collective-permute-start.5 = (bf16[256,128]{1,0:T(8,128)(2,1)S(1)}, bf16[256,128]{1,0:T(8,128)(2,1)}, u32[]{:S(2)}, u32[]{:S(2)}) collective-permute-start(bf16[256,128]{1,0:T(8,128)(2,1)S(1)} %slice_select_fusion.1), channel_id=1, source_target_pairs={{0,8},{8,16},{16,24},{24,0},{1,9},{9,17},{17,25},{25,1},{2,10},{10... | collective-permute-start | bytes 196616 | tf_op jit(solution)/shard_map/ppermute | solution.py:18
  39.6 13.2 %all_gather.7 = bf16[384,128]{1,0:T(8,128)(2,1)S(1)} all-gather(bf16[96,128]{1,0:T(8,128)(2,1)S(1)} %pad_maximum_fusion.1), channel_id=1, replica_groups=mesh['parts'=1,'ctx'=4,'pb'=4,'row'=2] {'ctx'}, dimensions={0}, use_global_device_ids=true | all-gather | bytes 122880 | tf_op jit(solution)/shard_map/all_gather | solution.py:97
  52.8 0.8 maximum_convert_fusion
  53.8 0.7 maximum_convert_fusion.1
  55.5 13.6 %all_gather.6 = bf16[384,192]{1,0:T(8,128)(2,1)S(1)} all-gather(bf16[96,192]{1,0:T(8,128)(2,1)S(1)} %pad_maximum_fusion), channel_id=1, replica_groups=mesh['parts'=1,'ctx'=4,'pb'=4,'row'=2] {'ctx'}, dimensions={0}, use_global_device_ids=true | all-gather | bytes 184320 | tf_op jit(solution)/shard_map/all_gather | solution.py:96
  70.6 3.7 %all-to-all-start.1 = ((bf16[1,4,4,64,192]{4,3,1,0,2:T(8,128)(2,1)}), bf16[1,4,4,64,192]{4,3,1,0,2:T(8,128)(2,1)S(1)}, u32[]{:S(2)}, u32[]{:S(2)}) async-start(bf16[1,4,4,64,192]{4,3,1,0,2:T(8,128)(2,1)} %copy_select_fusion), calls=%async_computation.1 | async-start | bytes 1048576 | tf_op jit(solution)/shard_map/all_to_all | solution.py:149
  74.3 1.7 %fusion.59 = (f32[1024]{0:T(1024)S(1)}, f32[1024,320]{0,1:T(8,128)S(1)}) fusion(bf16[1024,192]{1,0:T(8,128)(2,1)S(1)} %reshape.297, s32[]{:T(128)S(6)} %select_n.211, bf16[256,192]{0,1:T(8,128)(2,1)} %collective-permute-done.4, bf16[512,192]{0,1:T(8,128)(2,1)S(1)} %copy-done.2, s32[1024]{0:T(1024)S(1)} %broadcast_add_fusion, s32[1024]{0:T(1024)S(1)} %fusion.31, ...), kind=kOutput, calls=%fused_computation.137 | convolution fusion | flops 128039936 | bytes 2012420 | tf_op jit(solution)/shard_map/dot_general | solution.py:31
  76.4 1.5 %convolution_divide_fusion = f32[1024,128]{1,0:T(8,128)S(1)} fusion(f32[1024,320]{0,1:T(8,128)S(1)} %get-tuple-element.29, f32[1024]{0:T(1024)S(1)} %get-tuple-element.28, s32[1024]{0:T(1024)S(1)} %broadcast_add_fusion, s32[1024]{0:T(1024)S(1)} %fusion.31, s32[320]{0:T(512)S(1)} %iota_add_fusion.1, f32[1024]{0:T(1024)S(1)} %fusion.11, s32[]{:T(128)S(6)} %select_n.211, ...), kind=kOutput, calls=%fused_computation.21 | convolution fusion | flops 86147072 | bytes 2049284 | tf_op jit(solution)/shard_map/dot_general | solution.py:36
  78.0 6.4 %all-to-all-done.1 = bf16[1,4,4,64,192]{4,3,1,0,2:T(8,128)(2,1)S(1)} async-done(((bf16[1,4,4,64,192]{4,3,1,0,2:T(8,128)(2,1)}), bf16[1,4,4,64,192]{4,3,1,0,2:T(8,128)(2,1)S(1)}, u32[]{:S(2)}, u32[]{:S(2)}) %all-to-all-start.1) | async-done | bytes 393248 | tf_op jit(solution)/shard_map/all_to_all | solution.py:149
  84.4 1.2 %fusion = (f32[1024]{0:T(1024)S(1)}, f32[1024,1024]{1,0:T(8,128)S(1)}) fusion(s32[1024]{0:T(1024)S(1)} %fusion.31, s32[1024]{0:T(1024)S(1)} %add.265, pred[1024]{0:T(1024)(128)(4,1)S(1)} %copy-done.11, bf16[1024,192]{1,0:T(8,128)(2,1)S(1)} %bitcast.97, bf16[1024,192]{1,0:T(8,128)(2,1)S(1)} %reshape.297), kind=kOutput, calls=%fused_computation.8 | convolution fusion | flops 407895040 | bytes 4994048 | tf_op jit(solution)/shard_map/dot_general | solution.py:31
  85.6 1.9 %fusion.52 = f32[1024]{0:T(1024)S(1)} fusion(f32[1024]{0:T(1024)S(1)} %get-tuple-element.30, f32[1024,1024]{1,0:T(8,128)S(1)} %get-tuple-element.31, s32[1024]{0:T(1024)S(1)} %fusion.31, s32[1024]{0:T(1024)S(1)} %add.265, pred[1024]{0:T(1024)(128)(4,1)S(1)} %copy-done.11), kind=kLoop, calls=%fused_computation.130 | loop fusion | flops 7339008 | bytes 4211712 | tf_op jit(solution)/shard_map/reduce_sum | solution.py:37
  87.5 1.8 %fusion.6 = f32[1024,128]{1,0:T(8,128)S(1)} fusion(bf16[1024,128]{1,0:T(8,128)(2,1)S(1)} %bitcast.98, f32[1024]{0:T(1024)S(1)} %fusion.52, f32[1024,1024]{1,0:T(8,128)S(1)} %get-tuple-element.31, f32[1024]{0:T(1024)S(1)} %get-tuple-element.30, s32[1024]{0:T(1024)S(1)} %fusion.31, s32[1024]{0:T(1024)S(1)} %add.265, pred[1024]{0:T(1024)(128)(4,1)S(1)} %copy-done.11), kind=kOutput, calls=%fused_computation.20 | convolution fusion | flops 275906560 | bytes 4998144 | tf_op jit(solution)/shard_map/dot_general | solution.py:36
  90.6 1.3 %fusion.25 = bf16[64,2048]{1,0:T(8,128)(2,1)} fusion(f32[64,2048]{1,0:T(8,128)S(1)} %reshape.305, f32[8,8,16,128]{3,2,1,0:T(8,128)S(1)} %bitcast.92, f32[64,2048]{1,0:T(8,128)S(1)} %reshape.304, f32[8,8,16,128]{3,2,1,0:T(8,128)S(1)} %bitcast.91, f32[64,2048]{1,0:T(8,128)S(1)} %reshape.298, f32[8,8,16,128]{3,2,1,0:T(8,128)S(1)} %bitcast.90), kind=kLoop, calls=%fused_computation.40 | loop fusion | flops 786432 | bytes 3407872 | tf_op jit(solution)/shard_map/convert_element_type | solution.py:190
  (115 shorter events, 17.3 us)
Async XLA Ops:
  0.0 22.7 %copy-start.1 = (bf16[1024,128]{1,0:T(8,128)(2,1)S(1)}, bf16[1024,128]{1,0:T(8,128)(2,1)}, u32[]{:S(2)}) copy-start(bf16[1024,128]{1,0:T(8,128)(2,1)} %param.12) | copy-start | bytes 786436
  0.0 22.7 %copy-start = (bf16[512,128]{1,0:T(8,128)(2,1)S(1)}, bf16[512,128]{1,0:T(8,128)(2,1)}, u32[]{:S(2)}) copy-start(bf16[512,128]{1,0:T(8,128)(2,1)} %param.14) | copy-start | bytes 393220
  0.0 22.7 %copy-start.7 = (f32[32,192]{1,0:T(8,128)S(1)}, f32[32,192]{1,0:T(8,128)}, u32[]{:S(2)}) copy-start(f32[32,192]{1,0:T(8,128)} %param.15) | copy-start | bytes 73732
  0.0 22.7 %copy-start.3 = (bf16[64,3072]{1,0:T(8,128)(2,1)S(1)}, bf16[64,3072]{1,0:T(8,128)(2,1)}, u32[]{:S(2)}) copy-start(bf16[64,3072]{1,0:T(8,128)(2,1)} %param.10) | copy-start | bytes 1179652
  0.0 23.4 %copy-start.8 = (f32[32,128]{1,0:T(8,128)S(1)}, f32[32,128]{1,0:T(8,128)}, u32[]{:S(2)}) copy-start(f32[32,128]{1,0:T(8,128)} %param.16) | copy-start | bytes 49156
  0.0 25.2 %copy-start.9 = (bf16[64,48]{0,1:T(8,128)(2,1)S(1)}, bf16[64,48]{0,1:T(8,128)(2,1)}, u32[]{:S(2)}) copy-start(bf16[64,48]{0,1:T(8,128)(2,1)} %param.17) | copy-start | bytes 18436
  3.0 49.8 %collective-permute-start = (bf16[16,192]{1,0:T(8,128)(2,1)}, bf16[16,192]{1,0:T(8,128)(2,1)}, u32[]{:S(2)}, u32[]{:S(2)}) collective-permute-start(bf16[16,192]{1,0:T(8,128)(2,1)} %get-tuple-element.13), channel_id=1, source_target_pairs={{0,24},{8,0},{16,8},{24,16},{1,25},{9,1},{17,9},{25,17},{2,26},{10... | collective-permute-start | bytes 18440 | tf_op jit(solution)/shard_map/ppermute | solution.py:18
  8.0 45.7 %collective-permute-start.1 = (bf16[16,192]{1,0:T(8,128)(2,1)}, bf16[16,192]{1,0:T(8,128)(2,1)}, u32[]{:S(2)}, u32[]{:S(2)}) collective-permute-start(bf16[16,192]{1,0:T(8,128)(2,1)} %get-tuple-element.14), channel_id=1, source_target_pairs={{0,24},{8,0},{16,8},{24,16},{1,25},{9,1},{17,9},{25,17},{2,26},{10... | collective-permute-start | bytes 18440 | tf_op jit(solution)/shard_map/ppermute | solution.py:18
  9.8 25.8 %collective-permute-start.2 = (bf16[16,128]{1,0:T(8,128)(2,1)}, bf16[16,128]{1,0:T(8,128)(2,1)}, u32[]{:S(2)}, u32[]{:S(2)}) collective-permute-start(bf16[16,128]{1,0:T(8,128)(2,1)} %get-tuple-element.15), channel_id=1, source_target_pairs={{0,24},{8,0},{16,8},{24,16},{1,25},{9,1},{17,9},{25,17},{2,26},{10... | collective-permute-start | bytes 12296 | tf_op jit(solution)/shard_map/ppermute | solution.py:18
  10.2 28.2 %collective-permute-start.3 = (bf16[16,128]{1,0:T(8,128)(2,1)}, bf16[16,128]{1,0:T(8,128)(2,1)}, u32[]{:S(2)}, u32[]{:S(2)}) collective-permute-start(bf16[16,128]{1,0:T(8,128)(2,1)} %get-tuple-element.16), channel_id=1, source_target_pairs={{0,24},{8,0},{16,8},{24,16},{1,25},{9,1},{17,9},{25,17},{2,26},{10... | collective-permute-start | bytes 12296 | tf_op jit(solution)/shard_map/ppermute | solution.py:18
  13.7 13.6 %all-to-all-start = ((s32[1,4,4]{1,0,2:T(1,128)}), s32[1,4,4]{1,0,2:T(1,128)S(1)}, u32[]{:S(2)}, u32[]{:S(2)}) async-start(s32[1,4,4]{1,0,2:T(1,128)} %copy.85), calls=%async_computation | async-start | bytes 4096 | tf_op jit(solution)/shard_map/all_to_all | solution.py:132
  19.9 54.4 %collective-permute-start.4 = (bf16[256,192]{0,1:T(8,128)(2,1)S(1)}, bf16[256,192]{0,1:T(8,128)(2,1)}, u32[]{:S(2)}, u32[]{:S(2)}) collective-permute-start(bf16[256,192]{0,1:T(8,128)(2,1)S(1)} %slice_select_fusion), channel_id=1, source_target_pairs={{0,8},{8,16},{16,24},{24,0},{1,9},{9,17},{17,25},{25,1},{2,10},{10... | collective-permute-start | bytes 294920 | tf_op jit(solution)/shard_map/ppermute | solution.py:18
  31.1 39.6 %all-to-all-start.2 = ((bf16[1,4,4,64,128]{4,3,1,0,2:T(8,128)(2,1)}), bf16[1,4,4,64,128]{4,3,1,0,2:T(8,128)(2,1)S(1)}, u32[]{:S(2)}, u32[]{:S(2)}) async-start(bf16[1,4,4,64,128]{4,3,1,0,2:T(8,128)(2,1)} %copy.95), calls=%async_computation.2 | async-start | bytes 524288 | tf_op jit(solution)/shard_map/all_to_all | solution.py:150
  35.6 40.8 %collective-permute-start.5 = (bf16[256,128]{1,0:T(8,128)(2,1)S(1)}, bf16[256,128]{1,0:T(8,128)(2,1)}, u32[]{:S(2)}, u32[]{:S(2)}) collective-permute-start(bf16[256,128]{1,0:T(8,128)(2,1)S(1)} %slice_select_fusion.1), channel_id=1, source_target_pairs={{0,8},{8,16},{16,24},{24,0},{1,9},{9,17},{17,25},{25,1},{2,10},{10... | collective-permute-start | bytes 196616 | tf_op jit(solution)/shard_map/ppermute | solution.py:18
  54.6 14.4 %copy-start.10 = (s32[384]{0:T(512)S(1)}, s32[384]{0:T(512)}, u32[]{:S(2)}) copy-start(s32[384]{0:T(512)} %multiply_add_fusion) | copy-start | bytes 4612
  70.5 3.8 %copy-start.2 = (bf16[512,192]{0,1:T(8,128)(2,1)S(1)}, bf16[512,192]{0,1:T(8,128)(2,1)}, u32[]{:S(2)}) copy-start(bf16[512,192]{0,1:T(8,128)(2,1)} %param.13) | copy-start | bytes 589828
  70.6 13.7 %all-to-all-start.1 = ((bf16[1,4,4,64,192]{4,3,1,0,2:T(8,128)(2,1)}), bf16[1,4,4,64,192]{4,3,1,0,2:T(8,128)(2,1)S(1)}, u32[]{:S(2)}, u32[]{:S(2)}) async-start(bf16[1,4,4,64,192]{4,3,1,0,2:T(8,128)(2,1)} %copy_select_fusion), calls=%async_computation.1 | async-start | bytes 1048576 | tf_op jit(solution)/shard_map/all_to_all | solution.py:149
  77.9 6.5 %copy-start.11 = (pred[1024]{0:T(1024)(128)(4,1)S(1)}, pred[1024]{0:T(1024)(128)(4,1)}, u32[]{:S(2)}) copy-start(pred[1024]{0:T(1024)(128)(4,1)} %and.99) | copy-start | bytes 3076
  87.5 2.0 %copy-start.4 = (f32[64,16]{1,0:T(8,128)S(1)}, f32[64,16]{1,0:T(8,128)}, u32[]{:S(2)}) copy-start(f32[64,16]{1,0:T(8,128)} %copy.76) | copy-start | bytes 12292
  89.4 0.8 copy-start.5
  89.4 0.9 %copy-start.6 = (f32[64,16]{1,0:T(8,128)S(1)}, f32[64,16]{1,0:T(8,128)}, u32[]{:S(2)}) copy-start(f32[64,16]{1,0:T(8,128)} %copy.97) | copy-start | bytes 12292
where the time goes:
time: 92.6 us; the launch traced here: 91.8 us
  blocking collectives  26.8 us (29%)
  starting transfers between devices  22.7 us (25%)
  other arithmetic  14.1 us (15%)
  local copies, waits for them, and re-layouts  13.3 us (14%)
  matrix products  7.31 us (8%)
  waiting for transfers between devices  6.38 us (7%)
  between operations  1.25 us (1%)
    all_gather x1, blocking collectives, local(): part_keys = lax.all_gather(summary_keys, 'ctx', axis=0, tiled=True)  13.6 us
    all_gather x1, blocking collectives, local(): part_values = lax.all_gather(summary_values, 'ctx', axis=0, tiled=True)  13.2 us
    ppermute x6, starting transfers between devices, from_behind(): return lax.ppermute(value, axis, pairs)  10.1 us
    all_to_all x1, waiting for transfers between devices, local(): lax.all_to_all(served_keys, 'ctx', split_axis=2, concat_axis=2, tiled=True)  6.36 us
    all_to_all x1, starting transfers between devices, local(): lax.all_to_all(requested, 'ctx', split_axis=2, concat_axis=2, tiled=True)  5.27 us
    all_to_all x1, starting transfers between devices, local(): lax.all_to_all(served_keys, 'ctx', split_axis=2, concat_axis=2, tiled=True)  3.66 us
    all_to_all x1, starting transfers between devices, local(): lax.all_to_all(served_values, 'ctx', split_axis=2, concat_axis=2, tiled=T...  3.63 us
    unnamed x27, local copies, waits for them, and re-layouts  3.33 us
  transfers between devices with their start and end apart: 9, of which 1 were waited for; matrix products, arithmetic and copies ran while one was open for 27% of the time, Pallas kernels for 0%

commit v1 on v0

--- a/solution.py
+++ b/solution.py
@@ -93,8 +93,13 @@
     running_max = jnp.full((row_count,), NEG_FILL, jnp.float32)
     running_sum = jnp.zeros((row_count,), jnp.float32)
     running_out = jnp.zeros((row_count, value_width), jnp.float32)
-    part_keys = lax.all_gather(summary_keys, "ctx", axis=0, tiled=True)
-    part_values = lax.all_gather(summary_values, "ctx", axis=0, tiled=True)
+    part_keys, part_values = jnp.split(
+        lax.all_gather(
+            jnp.concatenate([summary_keys, summary_values], axis=1), "ctx", axis=0, tiled=True
+        ),
+        [summary_keys.shape[1]],
+        axis=1,
+    )
     length = part_keys.shape[0]
     for lower_row in range(0, length, 512):
         upper_row = min(lower_row + 512, length)

time: 92.6 us -> 79.8 us (0.86)
  blocking collectives: 26.8 us -> 13.9 us
    all_gather x2 -> x1, blocking collectives: 26.8 us -> 13.9 us  [local(): lax.all_gather(jnp.concatenate([summary_keys, summary_values], axis=1), '...]
  transfers between devices with their start and end apart: 9 -> 9, of which waited for: 1 -> 1; matrix products, arithmetic and copies ran while one was open for 27% -> 31% of each run, Pallas kernels for 0% -> 0%
where the time goes in v1:
time: 79.8 us; the launch traced here: 79.1 us
  starting transfers between devices  22.7 us (28%)
  other arithmetic  14.2 us (18%)
  blocking collectives  13.9 us (17%)
  local copies, waits for them, and re-layouts  13.3 us (17%)
  matrix products  7.39 us (9%)
  waiting for transfers between devices  6.38 us (8%)
  between operations  1.24 us (2%)
    all_gather x1, blocking collectives, local(): lax.all_gather(jnp.concatenate([summary_keys, summary_values], axis=1), '...  13.9 us
    ppermute x6, starting transfers between devices, from_behind(): return lax.ppermute(value, axis, pairs)  10.1 us
    all_to_all x1, waiting for transfers between devices, local(): lax.all_to_all(served_keys, 'ctx', split_axis=2, concat_axis=2, tiled=True)  6.36 us
    all_to_all x1, starting transfers between devices, local(): lax.all_to_all(requested, 'ctx', split_axis=2, concat_axis=2, tiled=True)  5.27 us
    all_to_all x1, starting transfers between devices, local(): lax.all_to_all(served_keys, 'ctx', split_axis=2, concat_axis=2, tiled=True)  3.66 us
    all_to_all x1, starting transfers between devices, local(): lax.all_to_all(served_values, 'ctx', split_axis=2, concat_axis=2, tiled=T...  3.63 us
    unnamed x27, local copies, waits for them, and re-layouts  3.33 us
    dot_general x2, matrix products, attend(): numerator = jnp.dot(weights, values, preferred_element_type=jnp.float32)  3.33 us
  transfers between devices with their start and end apart: 9, of which 1 were waited for; matrix products, arithmetic and copies ran while one was open for 31% of the time, Pallas kernels for 0%

profile of v1, /device:TPU:0, one launch (start us, length us, event | category | flops | bytes accessed | tf_op | source)
XLA Modules:
  0.0 79.1 jit_solution(2158337222110354219)
XLA Ops:
  0.0 1.3 %copy.79 = bf16[1024,192]{1,0:T(8,128)(2,1)S(1)} copy(bf16[1024,192]{0,1:T(8,128)(2,1)} %param.11) | data formatting | bytes 786432 | tf_op args[1]
  1.3 1.1 %copy.77 = bf16[512,192]{1,0:T(8,128)(2,1)S(1)} copy(bf16[512,192]{0,1:T(8,128)(2,1)} %param.13) | data formatting | bytes 393216 | tf_op args[3]
  3.0 5.1 %collective-permute-start = (bf16[16,192]{1,0:T(8,128)(2,1)}, bf16[16,192]{1,0:T(8,128)(2,1)}, u32[]{:S(2)}, u32[]{:S(2)}) collective-permute-start(bf16[16,192]{1,0:T(8,128)(2,1)} %get-tuple-element.13), channel_id=1, source_target_pairs={{0,24},{8,0},{16,8},{24,16},{1,25},{9,1},{17,9},{25,17},{2,26},{10... | collective-permute-start | bytes 18440 | tf_op jit(solution)/shard_map/ppermute | solution.py:18
  8.5 1.3 %slice_select_fusion.3 = (bf16[16,128]{1,0:T(8,128)(2,1)}, bf16[16,128]{1,0:T(8,128)(2,1)}) fusion(bf16[1024,128]{1,0:T(8,128)(2,1)} %param.12, pred[]{:T(512)S(6)} %eq.10, bf16[512,128]{1,0:T(8,128)(2,1)} %param.14), kind=kLoop, calls=%fused_computation.89 | loop fusion | flops 2048 | bytes 16385 | tf_op jit(solution)/shard_map/jit(_where)/select_n | solution.py:70
  10.8 1.3 %reduce.3 = s32[16]{0:T(128)S(1)} reduce(s32[1,16]{1,0:T(1,128)} %param.18, s32[]{:T(128)} %broadcast.494), dimensions={0}, to_apply=%param.18.reduce_sub_computation.3 | reduce | bytes 132 | tf_op args[8]
  13.7 5.3 %all-to-all-start = ((s32[1,4,4]{1,0,2:T(1,128)}), s32[1,4,4]{1,0,2:T(1,128)S(1)}, u32[]{:S(2)}, u32[]{:S(2)}) async-start(s32[1,4,4]{1,0,2:T(1,128)} %copy.85), calls=%async_computation | async-start | bytes 4096 | tf_op jit(solution)/shard_map/all_to_all | solution.py:137
  18.9 1.0 %slice_select_fusion = bf16[256,192]{0,1:T(8,128)(2,1)S(1)} fusion(bf16[512,192]{0,1:T(8,128)(2,1)} %param.13, bf16[1024,192]{0,1:T(8,128)(2,1)} %param.11, pred[]{:T(512)S(6)} %eq.11), kind=kLoop, calls=%fused_computation.62 | loop fusion | flops 49152 | bytes 294913 | tf_op jit(solution)/shard_map/jit(_where)/select_n | solution.py:160
  19.9 2.1 %collective-permute-start.4 = (bf16[256,192]{0,1:T(8,128)(2,1)S(1)}, bf16[256,192]{0,1:T(8,128)(2,1)}, u32[]{:S(2)}, u32[]{:S(2)}) collective-permute-start(bf16[256,192]{0,1:T(8,128)(2,1)S(1)} %slice_select_fusion), channel_id=1, source_target_pairs={{0,8},{8,16},{16,24},{24,0},{1,9},{9,17},{17,25},{25,1},{2,10},{10... | collective-permute-start | bytes 294920 | tf_op jit(solution)/shard_map/ppermute | solution.py:18
  30.4 0.7 copy.95
  31.1 3.6 %all-to-all-start.2 = ((bf16[1,4,4,64,128]{4,3,1,0,2:T(8,128)(2,1)}), bf16[1,4,4,64,128]{4,3,1,0,2:T(8,128)(2,1)S(1)}, u32[]{:S(2)}, u32[]{:S(2)}) async-start(bf16[1,4,4,64,128]{4,3,1,0,2:T(8,128)(2,1)} %copy.95), calls=%async_computation.2 | async-start | bytes 524288 | tf_op jit(solution)/shard_map/all_to_all | solution.py:155
  34.7 0.9 %copy_select_fusion = bf16[1,4,4,64,192]{4,3,1,0,2:T(8,128)(2,1)} fusion(bf16[1,4,4,64,192]{4,3,2,1,0:T(8,128)(2,1)S(1)} %bitcast.87, bf16[1,4,4,64,192]{4,3,2,1,0:T(8,128)(2,1)S(1)} %bitcast.86, pred[4,4]{0,1:T(4,128)(4,1)S(1)} %copy.87), kind=kLoop, calls=%fused_computation.44 | loop fusion | flops 196608 | bytes 1179664 | tf_op jit(solution)/shard_map/jit(_where)/select_n | solution.py:143
  35.6 2.0 %collective-permute-start.5 = (bf16[256,128]{1,0:T(8,128)(2,1)S(1)}, bf16[256,128]{1,0:T(8,128)(2,1)}, u32[]{:S(2)}, u32[]{:S(2)}) collective-permute-start(bf16[256,128]{1,0:T(8,128)(2,1)S(1)} %slice_select_fusion.1), channel_id=1, source_target_pairs={{0,8},{8,16},{16,24},{24,0},{1,9},{9,17},{17,25},{25,1},{2,10},{10... | collective-permute-start | bytes 196616 | tf_op jit(solution)/shard_map/ppermute | solution.py:18
  39.6 0.8 maximum_convert_fusion
  40.5 0.7 maximum_convert_fusion.1
  42.3 13.9 %all_gather.3 = bf16[384,320]{1,0:T(8,128)(2,1)S(1)} all-gather(bf16[96,320]{1,0:T(8,128)(2,1)S(1)} %maximum_maximum_fusion), channel_id=1, replica_groups=mesh['parts'=1,'ctx'=4,'pb'=4,'row'=2] {'ctx'}, dimensions={0}, use_global_device_ids=true | all-gather | bytes 307200 | tf_op jit(solution)/shard_map/all_gather | solution.py:97
  57.0 0.8 fusion.5
  57.9 3.7 %all-to-all-start.1 = ((bf16[1,4,4,64,192]{4,3,1,0,2:T(8,128)(2,1)}), bf16[1,4,4,64,192]{4,3,1,0,2:T(8,128)(2,1)S(1)}, u32[]{:S(2)}, u32[]{:S(2)}) async-start(bf16[1,4,4,64,192]{4,3,1,0,2:T(8,128)(2,1)} %copy_select_fusion), calls=%async_computation.1 | async-start | bytes 1048576 | tf_op jit(solution)/shard_map/all_to_all | solution.py:154
  61.6 1.7 %fusion.61 = (f32[1024]{0:T(1024)S(1)}, f32[1024,320]{0,1:T(8,128)S(1)}) fusion(bf16[1024,192]{1,0:T(8,128)(2,1)S(1)} %reshape.297, s32[]{:T(128)S(6)} %select_n.211, bf16[256,192]{0,1:T(8,128)(2,1)} %collective-permute-done.4, bf16[512,192]{0,1:T(8,128)(2,1)S(1)} %copy-done.2, s32[1024]{0:T(1024)S(1)} %broadcast_add_fusion, s32[1024]{0:T(1024)S(1)} %fusion.33, ...), kind=kOutput, calls=%fused_computation.138 | convolution fusion | flops 128039936 | bytes 2012420 | tf_op jit(solution)/shard_map/dot_general | solution.py:31
  63.6 1.5 %convolution_divide_fusion = f32[1024,128]{1,0:T(8,128)S(1)} fusion(f32[1024,320]{0,1:T(8,128)S(1)} %get-tuple-element.29, f32[1024]{0:T(1024)S(1)} %get-tuple-element.28, s32[1024]{0:T(1024)S(1)} %broadcast_add_fusion, s32[1024]{0:T(1024)S(1)} %fusion.33, s32[320]{0:T(512)S(1)} %iota_add_fusion.1, f32[1024]{0:T(1024)S(1)} %fusion.11, s32[]{:T(128)S(6)} %select_n.211, ...), kind=kOutput, calls=%fused_computation.21 | convolution fusion | flops 86147072 | bytes 2049284 | tf_op jit(solution)/shard_map/dot_general | solution.py:36
  65.3 6.4 %all-to-all-done.1 = bf16[1,4,4,64,192]{4,3,1,0,2:T(8,128)(2,1)S(1)} async-done(((bf16[1,4,4,64,192]{4,3,1,0,2:T(8,128)(2,1)}), bf16[1,4,4,64,192]{4,3,1,0,2:T(8,128)(2,1)S(1)}, u32[]{:S(2)}, u32[]{:S(2)}) %all-to-all-start.1) | async-done | bytes 393248 | tf_op jit(solution)/shard_map/all_to_all | solution.py:154
  71.7 1.2 %fusion = (f32[1024]{0:T(1024)S(1)}, f32[1024,1024]{1,0:T(8,128)S(1)}) fusion(s32[1024]{0:T(1024)S(1)} %fusion.33, s32[1024]{0:T(1024)S(1)} %add.265, pred[1024]{0:T(1024)(128)(4,1)S(1)} %copy-done.11, bf16[1024,192]{1,0:T(8,128)(2,1)S(1)} %bitcast.95, bf16[1024,192]{1,0:T(8,128)(2,1)S(1)} %reshape.297), kind=kOutput, calls=%fused_computation.8 | convolution fusion | flops 407895040 | bytes 4994048 | tf_op jit(solution)/shard_map/dot_general | solution.py:31
  72.9 1.9 %fusion.54 = f32[1024]{0:T(1024)S(1)} fusion(f32[1024]{0:T(1024)S(1)} %get-tuple-element.30, f32[1024,1024]{1,0:T(8,128)S(1)} %get-tuple-element.31, s32[1024]{0:T(1024)S(1)} %fusion.33, s32[1024]{0:T(1024)S(1)} %add.265, pred[1024]{0:T(1024)(128)(4,1)S(1)} %copy-done.11), kind=kLoop, calls=%fused_computation.131 | loop fusion | flops 7339008 | bytes 4211712 | tf_op jit(solution)/shard_map/reduce_sum | solution.py:37
  74.8 1.8 %fusion.6 = f32[1024,128]{1,0:T(8,128)S(1)} fusion(bf16[1024,128]{1,0:T(8,128)(2,1)S(1)} %bitcast.96, f32[1024]{0:T(1024)S(1)} %fusion.54, f32[1024,1024]{1,0:T(8,128)S(1)} %get-tuple-element.31, f32[1024]{0:T(1024)S(1)} %get-tuple-element.30, s32[1024]{0:T(1024)S(1)} %fusion.33, s32[1024]{0:T(1024)S(1)} %add.265, pred[1024]{0:T(1024)(128)(4,1)S(1)} %copy-done.11), kind=kOutput, calls=%fused_computation.20 | convolution fusion | flops 275906560 | bytes 4998144 | tf_op jit(solution)/shard_map/dot_general | solution.py:36
  77.8 1.3 %fusion.25 = bf16[64,2048]{1,0:T(8,128)(2,1)} fusion(f32[64,2048]{1,0:T(8,128)S(1)} %reshape.305, f32[8,8,16,128]{3,2,1,0:T(8,128)S(1)} %bitcast.90, f32[64,2048]{1,0:T(8,128)S(1)} %reshape.304, f32[8,8,16,128]{3,2,1,0:T(8,128)S(1)} %bitcast.89, f32[64,2048]{1,0:T(8,128)S(1)} %reshape.298, f32[8,8,16,128]{3,2,1,0:T(8,128)S(1)} %bitcast.88), kind=kLoop, calls=%fused_computation.40 | loop fusion | flops 786432 | bytes 3407872 | tf_op jit(solution)/shard_map/convert_element_type | solution.py:195
  (113 shorter events, 16.7 us)
Async XLA Ops:
  0.0 22.7 %copy-start.1 = (bf16[1024,128]{1,0:T(8,128)(2,1)S(1)}, bf16[1024,128]{1,0:T(8,128)(2,1)}, u32[]{:S(2)}) copy-start(bf16[1024,128]{1,0:T(8,128)(2,1)} %param.12) | copy-start | bytes 786436
  0.0 22.7 %copy-start = (bf16[512,128]{1,0:T(8,128)(2,1)S(1)}, bf16[512,128]{1,0:T(8,128)(2,1)}, u32[]{:S(2)}) copy-start(bf16[512,128]{1,0:T(8,128)(2,1)} %param.14) | copy-start | bytes 393220
  0.0 22.7 %copy-start.7 = (f32[32,192]{1,0:T(8,128)S(1)}, f32[32,192]{1,0:T(8,128)}, u32[]{:S(2)}) copy-start(f32[32,192]{1,0:T(8,128)} %param.15) | copy-start | bytes 73732
  0.0 22.7 %copy-start.8 = (f32[32,128]{1,0:T(8,128)S(1)}, f32[32,128]{1,0:T(8,128)}, u32[]{:S(2)}) copy-start(f32[32,128]{1,0:T(8,128)} %param.16) | copy-start | bytes 49156
  0.0 22.8 %copy-start.3 = (bf16[64,3072]{1,0:T(8,128)(2,1)S(1)}, bf16[64,3072]{1,0:T(8,128)(2,1)}, u32[]{:S(2)}) copy-start(bf16[64,3072]{1,0:T(8,128)(2,1)} %param.10) | copy-start | bytes 1179652
  0.0 25.2 %copy-start.9 = (bf16[64,48]{0,1:T(8,128)(2,1)S(1)}, bf16[64,48]{0,1:T(8,128)(2,1)}, u32[]{:S(2)}) copy-start(bf16[64,48]{0,1:T(8,128)(2,1)} %param.17) | copy-start | bytes 18436
  3.0 36.6 %collective-permute-start = (bf16[16,192]{1,0:T(8,128)(2,1)}, bf16[16,192]{1,0:T(8,128)(2,1)}, u32[]{:S(2)}, u32[]{:S(2)}) collective-permute-start(bf16[16,192]{1,0:T(8,128)(2,1)} %get-tuple-element.13), channel_id=1, source_target_pairs={{0,24},{8,0},{16,8},{24,16},{1,25},{9,1},{17,9},{25,17},{2,26},{10... | collective-permute-start | bytes 18440 | tf_op jit(solution)/shard_map/ppermute | solution.py:18
  8.0 32.5 %collective-permute-start.1 = (bf16[16,192]{1,0:T(8,128)(2,1)}, bf16[16,192]{1,0:T(8,128)(2,1)}, u32[]{:S(2)}, u32[]{:S(2)}) collective-permute-start(bf16[16,192]{1,0:T(8,128)(2,1)} %get-tuple-element.14), channel_id=1, source_target_pairs={{0,24},{8,0},{16,8},{24,16},{1,25},{9,1},{17,9},{25,17},{2,26},{10... | collective-permute-start | bytes 18440 | tf_op jit(solution)/shard_map/ppermute | solution.py:18
  9.8 25.8 %collective-permute-start.2 = (bf16[16,128]{1,0:T(8,128)(2,1)}, bf16[16,128]{1,0:T(8,128)(2,1)}, u32[]{:S(2)}, u32[]{:S(2)}) collective-permute-start(bf16[16,128]{1,0:T(8,128)(2,1)} %get-tuple-element.15), channel_id=1, source_target_pairs={{0,24},{8,0},{16,8},{24,16},{1,25},{9,1},{17,9},{25,17},{2,26},{10... | collective-permute-start | bytes 12296 | tf_op jit(solution)/shard_map/ppermute | solution.py:18
  10.2 28.2 %collective-permute-start.3 = (bf16[16,128]{1,0:T(8,128)(2,1)}, bf16[16,128]{1,0:T(8,128)(2,1)}, u32[]{:S(2)}, u32[]{:S(2)}) collective-permute-start(bf16[16,128]{1,0:T(8,128)(2,1)} %get-tuple-element.16), channel_id=1, source_target_pairs={{0,24},{8,0},{16,8},{24,16},{1,25},{9,1},{17,9},{25,17},{2,26},{10... | collective-permute-start | bytes 12296 | tf_op jit(solution)/shard_map/ppermute | solution.py:18
  13.7 13.6 %all-to-all-start = ((s32[1,4,4]{1,0,2:T(1,128)}), s32[1,4,4]{1,0,2:T(1,128)S(1)}, u32[]{:S(2)}, u32[]{:S(2)}) async-start(s32[1,4,4]{1,0,2:T(1,128)} %copy.85), calls=%async_computation | async-start | bytes 4096 | tf_op jit(solution)/shard_map/all_to_all | solution.py:137
  19.9 41.7 %collective-permute-start.4 = (bf16[256,192]{0,1:T(8,128)(2,1)S(1)}, bf16[256,192]{0,1:T(8,128)(2,1)}, u32[]{:S(2)}, u32[]{:S(2)}) collective-permute-start(bf16[256,192]{0,1:T(8,128)(2,1)S(1)} %slice_select_fusion), channel_id=1, source_target_pairs={{0,8},{8,16},{16,24},{24,0},{1,9},{9,17},{17,25},{25,1},{2,10},{10... | collective-permute-start | bytes 294920 | tf_op jit(solution)/shard_map/ppermute | solution.py:18
  31.1 26.8 %all-to-all-start.2 = ((bf16[1,4,4,64,128]{4,3,1,0,2:T(8,128)(2,1)}), bf16[1,4,4,64,128]{4,3,1,0,2:T(8,128)(2,1)S(1)}, u32[]{:S(2)}, u32[]{:S(2)}) async-start(bf16[1,4,4,64,128]{4,3,1,0,2:T(8,128)(2,1)} %copy.95), calls=%async_computation.2 | async-start | bytes 524288 | tf_op jit(solution)/shard_map/all_to_all | solution.py:155
  35.6 28.0 %collective-permute-start.5 = (bf16[256,128]{1,0:T(8,128)(2,1)S(1)}, bf16[256,128]{1,0:T(8,128)(2,1)}, u32[]{:S(2)}, u32[]{:S(2)}) collective-permute-start(bf16[256,128]{1,0:T(8,128)(2,1)S(1)} %slice_select_fusion.1), channel_id=1, source_target_pairs={{0,8},{8,16},{16,24},{24,0},{1,9},{9,17},{17,25},{25,1},{2,10},{10... | collective-permute-start | bytes 196616 | tf_op jit(solution)/shard_map/ppermute | solution.py:18
  41.4 14.8 %copy-start.10 = (s32[384]{0:T(512)S(1)}, s32[384]{0:T(512)}, u32[]{:S(2)}) copy-start(s32[384]{0:T(512)} %multiply_add_fusion) | copy-start | bytes 4612
  57.8 3.8 %copy-start.2 = (bf16[512,192]{0,1:T(8,128)(2,1)S(1)}, bf16[512,192]{0,1:T(8,128)(2,1)}, u32[]{:S(2)}) copy-start(bf16[512,192]{0,1:T(8,128)(2,1)} %param.13) | copy-start | bytes 589828
  57.9 13.7 %all-to-all-start.1 = ((bf16[1,4,4,64,192]{4,3,1,0,2:T(8,128)(2,1)}), bf16[1,4,4,64,192]{4,3,1,0,2:T(8,128)(2,1)S(1)}, u32[]{:S(2)}, u32[]{:S(2)}) async-start(bf16[1,4,4,64,192]{4,3,1,0,2:T(8,128)(2,1)} %copy_select_fusion), calls=%async_computation.1 | async-start | bytes 1048576 | tf_op jit(solution)/shard_map/all_to_all | solution.py:154
  65.1 6.5 %copy-start.11 = (pred[1024]{0:T(1024)(128)(4,1)S(1)}, pred[1024]{0:T(1024)(128)(4,1)}, u32[]{:S(2)}) copy-start(pred[1024]{0:T(1024)(128)(4,1)} %and.99) | copy-start | bytes 3076
  74.8 2.0 %copy-start.4 = (f32[64,16]{1,0:T(8,128)S(1)}, f32[64,16]{1,0:T(8,128)}, u32[]{:S(2)}) copy-start(f32[64,16]{1,0:T(8,128)} %copy.76) | copy-start | bytes 12292
  76.6 0.8 copy-start.5
  76.6 0.9 %copy-start.6 = (f32[64,16]{1,0:T(8,128)S(1)}, f32[64,16]{1,0:T(8,128)}, u32[]{:S(2)}) copy-start(f32[64,16]{1,0:T(8,128)} %copy.97) | copy-start | bytes 12292
